TPU v7x, 512 devices: a whole 4x8x8 slice. The times are simulated.
512 devices in a mesh: row: 16 (over y, core), col: 32 (over z, x).
Axes of the slice: x: 4, y: 8, z: 8, core: 2. Of those that a mesh axis runs over, the one named last changes fastest.
Arguments:
- old_vectors: float32 [8192, 4096], P('row', 'col'), may hold values from -6 to 6, as said below
- pole_values: float32 [8192], replicated, may hold values from 0 to 8192, as said below
- live_mask: int32 [8192], replicated, may hold values from 0 to 1, as said below
- position: int32 [8192], replicated, may hold values from 0 to 8191, as said below
- rank_weight: float32 [1], replicated, may hold values from 0.5 to 2
Outputs:
- new_vectors: float32 [8192, 8192], P('row', 'col')
Inputs may be any that keep to these rules, and one draw needn't show every extreme that they name: `pole_values`: strictly increasing; consecutive values differ by 0.2 or more. `old_vectors`: the entries of rows 4095 and 4096 have magnitude 0.5 to 1.5. Each merged position appears exactly once. In every aligned group of 16 consecutive columns s of the halves' eigenvectors (s = h * 4096 + m), exactly 12 have live_mask[position[s]] = 1.
All inputs are finite; a program needn't handle non-finite values.
Results may differ from a plain program's by a relative error of at most 0.0003.
Values sent between devices are 32-bit elements; how exact they have to be, the bound alone decides.
A program may use at most 64 MiB of HBM per device.

v0:
```python
import jax
import jax.numpy as jnp
from jax import lax
from jax.sharding import PartitionSpec as P

BISECT = 40


def bracket_lengths(pole_values, live_mask, squares, rank_value):
    order_size = pole_values.shape[0]
    positions = jnp.arange(order_size, dtype=jnp.int32)
    marked = jnp.where(live_mask > 0, positions, order_size)
    shifted = jnp.concatenate([marked[1:], jnp.full((1,), order_size, jnp.int32)])
    following = lax.cummin(shifted, axis=0, reverse=True)
    weight_sum = rank_value * jnp.sum(squares)
    next_gap = pole_values[jnp.minimum(following, order_size - 1)] - pole_values
    return jnp.where(following < order_size, next_gap, weight_sum)


def bisect_roots(pole_here, bracket_len, pole_values, squares, live_mask, rank_value):
    pole_diff = pole_values[None, :] - pole_here[:, None]
    alive_cols = (live_mask > 0)[None, :]

    def halving(interval, unused):
        low_end, high_end = interval
        middle = 0.5 * (low_end + high_end)
        offset_gap = pole_diff - middle[:, None]
        summands = jnp.where(
            alive_cols, squares[None, :] / jnp.where(alive_cols, offset_gap, 1.0), 0.0
        )
        secular = 1.0 + rank_value * jnp.sum(summands, axis=1)
        is_below = secular < 0.0
        return ((jnp.where(is_below, middle, low_end), jnp.where(is_below, high_end, middle)), None)

    interval, unused = lax.scan(
        halving, (jnp.zeros_like(bracket_len), bracket_len), None, length=BISECT
    )
    return 0.5 * (interval[0] + interval[1])


def log_terms(pole_here, offsets, live_here, own_index, pole_values, live_mask):
    order_size = pole_values.shape[0]
    pole_diff = pole_values[None, :] - pole_here[:, None]
    on_pole = own_index[:, None] == jnp.arange(order_size, dtype=jnp.int32)[None, :]
    quotient = jnp.where(
        on_pole, offsets[:, None], 1.0 - offsets[:, None] / jnp.where(on_pole, 1.0, pole_diff)
    )
    in_play = (live_here[:, None] > 0) & (live_mask[None, :] > 0)
    logs = jnp.where(in_play, jnp.log(jnp.abs(jnp.where(in_play, quotient, 1.0))), 0.0)
    return jnp.sum(logs, axis=0)


def column_norms(pole_here, offsets, live_here, pole_values, live_mask, hat_weights):
    alive_cols = (live_mask > 0)[None, :]
    offset_gap = pole_values[None, :] - pole_here[:, None] - offsets[:, None]
    summands = jnp.where(
        alive_cols, hat_weights[None, :] ** 2 / jnp.where(alive_cols, offset_gap, 1.0) ** 2, 0.0
    )
    return jnp.where(live_here > 0, jnp.sqrt(jnp.sum(summands, axis=1)), 1.0)


def cauchy_tile(
    sorted_rows,
    pole_cols,
    offset_cols,
    norm_cols,
    live_cols,
    col_index,
    pole_values,
    live_mask,
    hat_weights,
):
    row_poles = pole_values[sorted_rows]
    row_hats = hat_weights[sorted_rows]
    row_live = live_mask[sorted_rows] > 0
    col_live = (live_cols > 0)[None, :]
    both_live = row_live[:, None] & col_live
    offset_gap = row_poles[:, None] - pole_cols[None, :] - offset_cols[None, :]
    entries = row_hats[:, None] / jnp.where(both_live, offset_gap, 1.0) / norm_cols[None, :]
    identity = (sorted_rows[:, None] == col_index[None, :]).astype(jnp.float32)
    return jnp.where(col_live, jnp.where(both_live, entries, 0.0), identity)


def hat_from(log_sum, coupling, live_mask, rank_value):
    return jnp.where(
        live_mask > 0, jnp.sign(coupling) * jnp.exp(0.5 * (log_sum - jnp.log(rank_value))), 0.0
    )


def shards(old_vectors, pole_values, live_mask, position, rank_weight):
    rank_value = rank_weight[0]
    order_size = pole_values.shape[0]
    half_order = order_size // 2
    rows_here = old_vectors.shape[0]
    row_count = lax.axis_size("row")
    col_count = lax.axis_size("col")
    row_rank = lax.axis_index("row")
    col_rank = lax.axis_index("col")
    upper_owner = (half_order - 1) // rows_here
    lower_owner = half_order // rows_here
    edge_rows = jnp.stack(
        [
            jnp.where(row_rank == upper_owner, old_vectors[(half_order - 1) % rows_here], 0.0),
            jnp.where(row_rank == lower_owner, old_vectors[half_order % rows_here], 0.0),
        ]
    )
    edge_rows = lax.psum(edge_rows, "row")
    edge_rows = lax.all_gather(edge_rows, "col", axis=1, tiled=True)
    boundary = jnp.concatenate([edge_rows[0], edge_rows[1]])
    spread = jnp.zeros((order_size,), jnp.float32).at[position].set(boundary)
    coupling = jnp.where(live_mask > 0, spread, 0.0)
    squares = coupling * coupling
    bracket_len = bracket_lengths(pole_values, live_mask, squares, rank_value)
    block_cols = order_size // col_count
    per_device = block_cols // row_count
    block_first = col_rank * block_cols
    own_first = block_first + row_rank * per_device
    block_index = block_first + jnp.arange(block_cols, dtype=jnp.int32)
    own_poles = lax.dynamic_slice_in_dim(pole_values, own_first, per_device)
    own_live = lax.dynamic_slice_in_dim(live_mask, own_first, per_device)
    own_bracket = lax.dynamic_slice_in_dim(bracket_len, own_first, per_device)
    block_poles = lax.dynamic_slice_in_dim(pole_values, block_first, block_cols)
    block_live = lax.dynamic_slice_in_dim(live_mask, block_first, block_cols)
    bisected = bisect_roots(own_poles, own_bracket, pole_values, squares, live_mask, rank_value)
    own_offsets = jnp.where(own_live > 0, bisected, 0.5 * own_bracket)
    block_offsets = lax.all_gather(own_offsets, "row", axis=0, tiled=True)
    grouped = (
        block_poles.reshape(row_count, per_device),
        block_offsets.reshape(row_count, per_device),
        block_live.reshape(row_count, per_device),
        block_index.reshape(row_count, per_device),
    )

    def log_group(members):
        return log_terms(members[0], members[1], members[2], members[3], pole_values, live_mask)

    partial_logs = jnp.sum(lax.map(log_group, grouped), axis=0)
    log_sum = lax.psum(partial_logs, "col")
    hat_weights = hat_from(log_sum, coupling, live_mask, rank_value)

    def norm_group(members):
        return column_norms(members[0], members[1], members[2], pole_values, live_mask, hat_weights)

    block_norms = lax.map(norm_group, (grouped[0], grouped[1], grouped[2])).reshape(block_cols)
    half_id = row_rank * rows_here // half_order
    half_base = half_id * half_order
    panel_piece = lax.all_gather(old_vectors, "col", axis=1, tiled=True)
    sorted_rows = lax.dynamic_slice_in_dim(position, half_base, panel_piece.shape[1])
    cauchy = cauchy_tile(
        sorted_rows,
        block_poles,
        block_offsets,
        block_norms,
        block_live,
        block_index,
        pole_values,
        live_mask,
        hat_weights,
    )
    return jnp.dot(
        panel_piece, cauchy, precision=lax.Precision.HIGHEST, preferred_element_type=jnp.float32
    )


def solution(mesh):
    in_specs = (P("row", "col"), P(), P(), P(), P())
    out_specs = P("row", "col")
    return jax.shard_map(shards, mesh=mesh, in_specs=in_specs, out_specs=out_specs, check_vma=False)
```

profile of v0, /device:TPU:32, one launch (start us, length us, event | category | flops | bytes accessed | tf_op | source)
XLA Modules:
  0.0 492.8 jit_solution(11255109670068731941)
XLA Ops:
  6.5 0.7 all-gather.2.cloned.1.call-update
  7.3 0.7 broadcast_select_fusion.2
  8.0 23.6 %psum.14 = f32[2,128]{1,0:T(2,128)S(1)} all-reduce(f32[2,128]{1,0:T(2,128)S(1)} %pad_maximum_fusion.1), channel_id=1, replica_groups=mesh['row'=16,'col'=32] {'row'}, use_global_device_ids=true, to_apply=%region_0.1 | all-reduce | flops 256 | bytes 2048 | tf_op jit(solution)/shard_map/psum | solution.py:107
  31.5 49.0 %all_gather.9 = f32[2,4096]{1,0:T(2,128)S(1)} all-gather(f32[2,128]{1,0:T(2,128)S(1)} %psum.14), channel_id=1, replica_groups=mesh['row'=16,'col'=32] {'col'}, dimensions={1}, use_global_device_ids=true | all-gather | bytes 33792 | tf_op jit(solution)/shard_map/all_gather | solution.py:108
  80.6 0.8 compare_select_fusion.4
  81.4 30.5 %scatter_custom_fusion = f32[8192]{0:T(1024)S(1)} fusion(s32[8192]{0:T(1024)S(1)} %compare_select_fusion.4, f32[8192]{0:T(1024)S(1)} %pad_maximum_fusion, f32[]{:T(128)} %constant.114.clone.1), kind=kCustom, calls=%fused_computation.74 | custom fusion | bytes 32772 | tf_op jit(solution)/shard_map/scatter | solution.py:110
  111.9 1.4 fusion.44
  113.4 2.3 reduce-window.9
  116.8 0.8 broadcast_compare_fusion.4
  117.5 0.8 dynamic_slice.52
  118.3 45.5 %gather_fusion.1 = f32[8192]{0:T(1024)S(1)} fusion(f32[8192]{0:T(1024)S(1)} %copy-done, s32[8192]{0:T(1024)S(1)} %broadcast_clamp_fusion), kind=kCustom, calls=%fused_computation.1 | custom fusion | bytes 98304 | tf_op jit(solution)/shard_map/gather | solution.py:16
  165.1 46.3 %while.37 = (s32[]{:T(128)}, f32[16]{0:T(128)S(1)}, f32[16]{0:T(128)S(1)}, f32[]{:T(128)}, pred[1,8192]{1,0:T(4,128)(4,1)S(1)}, /*index=5*/f32[8192]{0:T(1024)S(...) while((s32[]{:T(128)}, f32[16]{0:T(128)S(1)}, ...), condition=%wide.region_7.8_spmd.clone, body=%wide.region_5.7_spmd.clone.sunk | while | flops 786563 | bytes 91005 | solution.py:35
  165.6 0.7 compare_select_fusion.10
  166.8 0.7 compare_select_fusion.10
  167.9 0.7 compare_select_fusion.10
  169.1 0.7 compare_select_fusion.10
  170.2 0.7 compare_select_fusion.10
  171.4 0.7 compare_select_fusion.10
  172.6 0.7 compare_select_fusion.10
  173.7 0.7 compare_select_fusion.10
  174.9 0.7 compare_select_fusion.10
  176.0 0.7 compare_select_fusion.10
  177.2 0.7 compare_select_fusion.10
  178.4 0.7 compare_select_fusion.10
  179.5 0.7 compare_select_fusion.10
  180.7 0.7 compare_select_fusion.10
  181.8 0.7 compare_select_fusion.10
  183.0 0.7 compare_select_fusion.10
  184.2 0.7 compare_select_fusion.10
  185.3 0.7 compare_select_fusion.10
  186.5 0.7 compare_select_fusion.10
  187.6 0.7 compare_select_fusion.10
  188.8 0.7 compare_select_fusion.10
  190.0 0.7 compare_select_fusion.10
  191.1 0.7 compare_select_fusion.10
  192.3 0.7 compare_select_fusion.10
  193.4 0.7 compare_select_fusion.10
  194.6 0.7 compare_select_fusion.10
  211.5 1.3 dynamic-slice
  213.6 23.5 %all-reduce = f32[256]{0:T(256)S(1)} all-reduce(f32[256]{0:T(256)S(1)} %fusion.40), channel_id=1, replica_groups=mesh['row'=16,'col'=32] {'row'}, use_global_device_ids=true, to_apply=%add | all-reduce | flops 256 | bytes 2048
  237.4 10.5 %while.35 = (s32[]{:T(128)}, f32[16,8192]{1,0:T(8,128)S(1)}, s32[16,16]{1,0:T(8,128)S(1)}, s32[8192]{0:T(1024)S(1)}, s32[16,16]{1,0:T(8,128)S(1)}, /*index=5*/f3...) while((s32[]{:T(128)}, f32[16,8192]{1,0:T(8,128)S(1)}, ...), condition=%wide.region_10.11_spmd, body=%wide.region_8.10_spmd.sunk | while | flops 1441810 | bytes 181013 | solution.py:137
  247.9 23.0 %gather_fusion = s32[4096]{0:T(1024)S(1)} fusion(s32[8192]{0:T(1024)S(1)} %get-tuple-element.538, s32[4096]{0:T(1024)S(1)} %get-tuple-element.264), kind=kCustom, calls=%fused_computation | custom fusion | bytes 49152 | tf_op jit(solution)/shard_map/gather | solution.py:75
  270.9 23.0 %gather_fusion.3 = f32[4096]{0:T(1024)S(1)} fusion(f32[8192]{0:T(1024)S(1)} %get-tuple-element.537, s32[4096]{0:T(1024)S(1)} %get-tuple-element.264), kind=kCustom, calls=%fused_computation.3 | custom fusion | bytes 49152 | tf_op jit(solution)/shard_map/gather | solution.py:73
  294.1 140.3 %psum.15 = f32[8192]{0:T(1024)S(1)} all-reduce(f32[8192]{0:T(1024)S(1)} %reduce_sum.48), channel_id=1, replica_groups=mesh['row'=16,'col'=32] {'col'}, use_global_device_ids=true, to_apply=%region_12.13 | all-reduce | flops 8192 | bytes 65536 | tf_op jit(solution)/shard_map/psum | solution.py:138
  434.5 23.0 %gather_fusion.2 = f32[4096]{0:T(1024)S(1)} fusion(f32[8192]{0:T(1024)S(1)} %get-tuple-element.267, s32[4096]{0:T(1024)S(1)} %get-tuple-element.264), kind=kCustom, calls=%fused_computation.2 | custom fusion | bytes 49152 | tf_op jit(solution)/shard_map/gather | solution.py:74
  457.5 8.1 %while.36 = (s32[]{:T(128)}, f32[16,16]{1,0:T(8,128)S(1)}, s32[16,16]{1,0:T(8,128)S(1)}, s32[8192]{0:T(1024)S(1)}, f32[1,8192]{1,0:T(1,128)S(1)}, /*index=5*/f32...) while((s32[]{:T(128)}, f32[16,16]{1,0:T(8,128)S(1)}, ...), condition=%wide.region_15.16_spmd, body=%wide.region_13.15_spmd.sunk | while | flops 925714 | bytes 115569 | solution.py:144
  465.7 19.3 %fusion.34 = f32[512,256]{0,1:T(8,128)S(1)} fusion(f32[512,4096]{1,0:T(8,128)} %all-gather.2.cloned.1.call-done, s32[256]{0:T(256)S(1)} %iota_add_fusion, f32[256]{0:T(256)S(1)} %div.58, f32[256]{0:T(256)S(1)} %all-reduce, f32[256]{0:T(256)S(1)} %dynamic_slice.52, f32[4096]{0:T(1024)S(1)} %gather_fusion.3, f32[4096]{0:T(1024)S(1)} %gather_fusion.2, ...), kind=kOutput, calls=%fused_computation.60 | convolution fusion | flops 6452936704 | bytes 8970496 | tf_op jit(solution)/shard_map/dot_general | solution.py:160
  485.0 1.0 copy.8
  (347 shorter events, 46.9 us)
Async XLA Ops:
  6.5 111.8 %copy-start = (f32[8192]{0:T(1024)S(1)}, f32[8192]{0:T(1024)}, u32[]{:S(2)}) copy-start(f32[8192]{0:T(1024)} %param.12) | copy-start | bytes 98308
  6.5 459.1 %all-gather.2.cloned.1.call-start = ((), (), s32[]{:S(2)}) async-start(), calls=%async_computation | async-start | bytes 8650752 | tf_op jit(solution)/shard_map/all_gather | solution.py:147
  118.3 95.1 %copy-start.1 = (s32[8192]{0:T(1024)S(1)}, s32[8192]{0:T(1024)}, u32[]{:S(2)}) copy-start(s32[8192]{0:T(1024)} %param.13) | copy-start | bytes 98308
  118.3 129.6 %copy-start.2 = (s32[8192]{0:T(1024)S(1)}, s32[8192]{0:T(1024)}, u32[]{:S(2)}) copy-start(s32[8192]{0:T(1024)} %param.14) | copy-start | bytes 98308
Sparse Core Ops, SparseCore 0:
  10.4 114.0 all-gather.1
where the time goes:
time: 494 us; the launch traced here: 493 us
  blocking collectives  236 us (48%)
  local copies, waits for them, and re-layouts  152 us (31%)
  other arithmetic  65.8 us (13%)
  matrix products  19.3 us (4%)
  between operations  15.6 us (3%)
    psum x1, blocking collectives, shards(): log_sum = lax.psum(partial_logs, 'col')  140 us
    all_gather x1, blocking collectives, shards(): edge_rows = lax.all_gather(edge_rows, 'col', axis=1, tiled=True)  49 us
    gather x1, local copies, waits for them, and re-layouts, bracket_lengths(): next_gap = pole_values[jnp.minimum(following, order_size - 1)] - pole_values  45.5 us
    scatter x1, local copies, waits for them, and re-layouts, shards(): spread = jnp.zeros((order_size,), jnp.float32).at[position].set(boundary)  30.5 us
    select_n x40, other arithmetic, halving(): jnp.where(is_below, high_end, middle)  26.3 us
    psum x1, blocking collectives, shards(): edge_rows = lax.psum(edge_rows, 'row')  23.6 us
    unnamed x1, blocking collectives  23.5 us
    gather x1, local copies, waits for them, and re-layouts, cauchy_tile(): row_live = live_mask[sorted_rows] > 0  23 us
  transfers between devices with their start and end apart: 1, of which 0 were waited for; matrix products, arithmetic and copies ran while one was open for 44% of the time, Pallas kernels for 0%

commit v1 on v0

--- a/solution.py
+++ b/solution.py
@@ -4,6 +4,13 @@
 from jax.sharding import PartitionSpec as P
 
 BISECT = 40
+
+
+def swapped_in(block, mesh_axis, dim):
+    size = lax.axis_size(mesh_axis)
+    blocks = jnp.stack([block for _ in range(size)])
+    blocks = lax.all_to_all(blocks, mesh_axis, split_axis=0, concat_axis=0)
+    return jnp.concatenate(blocks, axis=dim)
 
 
 def bracket_lengths(pole_values, live_mask, squares, rank_value):
@@ -105,7 +112,7 @@
         ]
     )
     edge_rows = lax.psum(edge_rows, "row")
-    edge_rows = lax.all_gather(edge_rows, "col", axis=1, tiled=True)
+    edge_rows = swapped_in(edge_rows, "col", 1)
     boundary = jnp.concatenate([edge_rows[0], edge_rows[1]])
     spread = jnp.zeros((order_size,), jnp.float32).at[position].set(boundary)
     coupling = jnp.where(live_mask > 0, spread, 0.0)

time: 494 us -> 461 us (0.933)
  blocking collectives: 236 us -> 190 us
  starting transfers between devices: 0.01 us -> 13.5 us
    all_gather x1 -> x0, blocking collectives: 49 us -> none  [shards(): edge_rows = lax.all_gather(edge_rows, 'col', axis=1, tiled=True)]
    all_to_all x0 -> x1, starting transfers between devices: none -> 13.5 us  [swapped_in(): blocks = lax.all_to_all(blocks, mesh_axis, split_axis=0, concat_axis=0)]
  transfers between devices with their start and end apart: 1 -> 2, of which waited for: 0 -> 0; matrix products, arithmetic and copies ran while one was open for 44% -> 47% of each run, Pallas kernels for 0% -> 0%
where the time goes in v1:
time: 461 us; the launch traced here: 460 us
  blocking collectives  190 us (41%)
  local copies, waits for them, and re-layouts  153 us (33%)
  other arithmetic  65.7 us (14%)
  matrix products  19.3 us (4%)
  between operations  15.6 us (3%)
  starting transfers between devices  13.5 us (3%)
    psum x1, blocking collectives, shards(): log_sum = lax.psum(partial_logs, 'col')  143 us
    gather x1, local copies, waits for them, and re-layouts, bracket_lengths(): next_gap = pole_values[jnp.minimum(following, order_size - 1)] - pole_values  45.5 us
    scatter x1, local copies, waits for them, and re-layouts, shards(): spread = jnp.zeros((order_size,), jnp.float32).at[position].set(boundary)  30.5 us
    select_n x40, other arithmetic, halving(): jnp.where(is_below, high_end, middle)  26.3 us
    psum x1, blocking collectives, shards(): edge_rows = lax.psum(edge_rows, 'row')  23.6 us
    unnamed x1, blocking collectives  23.5 us
    gather x1, local copies, waits for them, and re-layouts, cauchy_tile(): row_live = live_mask[sorted_rows] > 0  23 us
    gather x1, local copies, waits for them, and re-layouts, cauchy_tile(): row_poles = pole_values[sorted_rows]  23 us
  transfers between devices with their start and end apart: 2, of which 0 were waited for; matrix products, arithmetic and copies ran while one was open for 47% of the time, Pallas kernels for 0%

profile of v1, /device:TPU:32, one launch (start us, length us, event | category | flops | bytes accessed | tf_op | source)
XLA Modules:
  0.0 460.3 jit_solution(18235172250339332462)
XLA Ops:
  6.5 0.7 all-gather.2.cloned.1.call-update
  7.3 0.7 broadcast_select_fusion.2
  8.0 23.6 %psum.14 = f32[2,128]{1,0:T(2,128)S(1)} all-reduce(f32[2,128]{1,0:T(2,128)S(1)} %pad_maximum_fusion.1), channel_id=1, replica_groups=mesh['row'=16,'col'=32] {'row'}, use_global_device_ids=true, to_apply=%region_0.1 | all-reduce | flops 256 | bytes 2048 | tf_op jit(solution)/shard_map/psum | solution.py:114
  32.2 13.5 %all-to-all-start = ((f32[32,2,128]{2,1,0:T(2,128)}), f32[32,2,128]{2,1,0:T(2,128)S(1)}, u32[]{:S(2)}, u32[]{:S(2)}) async-start(f32[32,2,128]{2,1,0:T(2,128)} %stack.5), calls=%async_computation | async-start | bytes 65536 | tf_op jit(solution)/shard_map/all_to_all | solution.py:12
  45.8 0.8 compare_select_fusion.4
  46.5 0.8 broadcast_compare_fusion.4
  47.3 0.8 dynamic_slice.52
  48.1 0.7 fusion.37
  48.8 23.0 %gather_fusion = s32[4096]{0:T(1024)S(1)} fusion(s32[8192]{0:T(1024)S(1)} %copy-done.1, s32[4096]{0:T(1024)S(1)} %get-tuple-element.264), kind=kCustom, calls=%fused_computation | custom fusion | bytes 49152 | tf_op jit(solution)/shard_map/gather | solution.py:82
  71.9 23.0 %gather_fusion.3 = f32[4096]{0:T(1024)S(1)} fusion(f32[8192]{0:T(1024)S(1)} %copy-done, s32[4096]{0:T(1024)S(1)} %get-tuple-element.264), kind=kCustom, calls=%fused_computation.3 | custom fusion | bytes 49152 | tf_op jit(solution)/shard_map/gather | solution.py:80
  95.8 1.2 dynamic-slice
  97.6 30.5 %scatter_custom_fusion = f32[8192]{0:T(1024)S(1)} fusion(s32[8192]{0:T(1024)S(1)} %compare_select_fusion.4, f32[8192]{0:T(1024)S(1)} %pad_maximum_fusion, f32[]{:T(128)} %constant.114.clone.1), kind=kCustom, calls=%fused_computation.74 | custom fusion | bytes 32772 | tf_op jit(solution)/shard_map/scatter | solution.py:117
  128.9 2.3 reduce-window.9
  132.2 45.5 %gather_fusion.1 = f32[8192]{0:T(1024)S(1)} fusion(f32[8192]{0:T(1024)S(1)} %copy-done, s32[8192]{0:T(1024)S(1)} %broadcast_clamp_fusion), kind=kCustom, calls=%fused_computation.1 | custom fusion | bytes 98304 | tf_op jit(solution)/shard_map/gather | solution.py:23
  178.5 46.3 %while.37 = (s32[]{:T(128)}, f32[16]{0:T(128)S(1)}, f32[16]{0:T(128)S(1)}, f32[]{:T(128)}, pred[1,8192]{1,0:T(4,128)(4,1)S(1)}, /*index=5*/f32[8192]{0:T(1024)S(...) while((s32[]{:T(128)}, f32[16]{0:T(128)S(1)}, ...), condition=%wide.region_7.8_spmd.clone, body=%wide.region_5.7_spmd.clone.sunk | while | flops 786563 | bytes 91005 | solution.py:42
  178.9 0.7 compare_select_fusion.10
  180.1 0.7 compare_select_fusion.10
  181.3 0.7 compare_select_fusion.10
  182.4 0.7 compare_select_fusion.10
  183.6 0.7 compare_select_fusion.10
  184.7 0.7 compare_select_fusion.10
  185.9 0.7 compare_select_fusion.10
  187.1 0.7 compare_select_fusion.10
  188.2 0.7 compare_select_fusion.10
  189.4 0.7 compare_select_fusion.10
  190.5 0.7 compare_select_fusion.10
  191.7 0.7 compare_select_fusion.10
  192.8 0.7 compare_select_fusion.10
  194.0 0.7 compare_select_fusion.10
  195.2 0.7 compare_select_fusion.10
  196.3 0.7 compare_select_fusion.10
  197.5 0.7 compare_select_fusion.10
  198.6 0.7 compare_select_fusion.10
  199.8 0.7 compare_select_fusion.10
  201.0 0.7 compare_select_fusion.10
  202.1 0.7 compare_select_fusion.10
  203.3 0.7 compare_select_fusion.10
  204.4 0.7 compare_select_fusion.10
  205.6 0.7 compare_select_fusion.10
  206.8 0.7 compare_select_fusion.10
  210.2 0.7 compare_select_fusion.10
  225.0 23.5 %all-reduce = f32[256]{0:T(256)S(1)} all-reduce(f32[256]{0:T(256)S(1)} %fusion.40), channel_id=1, replica_groups=mesh['row'=16,'col'=32] {'row'}, use_global_device_ids=true, to_apply=%add | all-reduce | flops 256 | bytes 2048
  248.6 10.4 %while.35 = (s32[]{:T(128)}, f32[16,8192]{1,0:T(8,128)S(1)}, s32[16,16]{1,0:T(8,128)S(1)}, s32[8192]{0:T(1024)S(1)}, s32[16,16]{1,0:T(8,128)S(1)}, /*index=5*/f3...) while((s32[]{:T(128)}, f32[16,8192]{1,0:T(8,128)S(1)}, ...), condition=%wide.region_10.11_spmd, body=%wide.region_8.10_spmd.sunk | while | flops 1441810 | bytes 181013 | solution.py:144
  259.1 142.8 %psum.15 = f32[8192]{0:T(1024)S(1)} all-reduce(f32[8192]{0:T(1024)S(1)} %reduce_sum.48), channel_id=1, replica_groups=mesh['row'=16,'col'=32] {'col'}, use_global_device_ids=true, to_apply=%region_12.13 | all-reduce | flops 8192 | bytes 65536 | tf_op jit(solution)/shard_map/psum | solution.py:145
  401.9 23.0 %gather_fusion.2 = f32[4096]{0:T(1024)S(1)} fusion(f32[8192]{0:T(1024)S(1)} %get-tuple-element.267, s32[4096]{0:T(1024)S(1)} %get-tuple-element.264), kind=kCustom, calls=%fused_computation.2 | custom fusion | bytes 49152 | tf_op jit(solution)/shard_map/gather | solution.py:81
  425.0 8.1 %while.36 = (s32[]{:T(128)}, f32[16,16]{1,0:T(8,128)S(1)}, s32[16,16]{1,0:T(8,128)S(1)}, s32[8192]{0:T(1024)S(1)}, f32[1,8192]{1,0:T(1,128)S(1)}, /*index=5*/f32...) while((s32[]{:T(128)}, f32[16,16]{1,0:T(8,128)S(1)}, ...), condition=%wide.region_15.16_spmd, body=%wide.region_13.15_spmd.sunk | while | flops 925714 | bytes 115569 | solution.py:151
  433.1 19.3 %fusion.34 = f32[512,256]{0,1:T(8,128)S(1)} fusion(f32[512,4096]{1,0:T(8,128)} %all-gather.2.cloned.1.call-done, s32[256]{0:T(256)S(1)} %iota_add_fusion, f32[256]{0:T(256)S(1)} %div.58, f32[256]{0:T(256)S(1)} %all-reduce, f32[256]{0:T(256)S(1)} %dynamic_slice.52, f32[4096]{0:T(1024)S(1)} %gather_fusion.3, f32[4096]{0:T(1024)S(1)} %gather_fusion.2, ...), kind=kOutput, calls=%fused_computation.60 | convolution fusion | flops 6452936704 | bytes 8970496 | tf_op jit(solution)/shard_map/dot_general | solution.py:167
  452.4 1.0 copy.8
  (347 shorter events, 48.0 us)
Async XLA Ops:
  6.5 42.3 %copy-start.1 = (s32[8192]{0:T(1024)S(1)}, s32[8192]{0:T(1024)}, u32[]{:S(2)}) copy-start(s32[8192]{0:T(1024)} %param.13) | copy-start | bytes 98308
  6.5 426.6 %all-gather.2.cloned.1.call-start = ((), (), s32[]{:S(2)}) async-start(), calls=%async_computation.1 | async-start | bytes 8650752 | tf_op jit(solution)/shard_map/all_gather | solution.py:154
  32.2 65.4 %all-to-all-start = ((f32[32,2,128]{2,1,0:T(2,128)}), f32[32,2,128]{2,1,0:T(2,128)S(1)}, u32[]{:S(2)}, u32[]{:S(2)}) async-start(f32[32,2,128]{2,1,0:T(2,128)} %stack.5), calls=%async_computation | async-start | bytes 65536 | tf_op jit(solution)/shard_map/all_to_all | solution.py:12
  48.8 23.1 %copy-start = (f32[8192]{0:T(1024)S(1)}, f32[8192]{0:T(1024)}, u32[]{:S(2)}) copy-start(f32[8192]{0:T(1024)} %param.12) | copy-start | bytes 98308
Sparse Core Ops, SparseCore 0:
  10.4 114.1 all-gather.1
